TPU v7x, 32 devices: a whole 2x2x4 slice. The times are simulated.
32 devices in a mesh: seq: 16 (over z, y, core), fsdp: 2 (over x).
Axes of the slice: x: 2, y: 2, z: 4, core: 2. Of those that a mesh axis runs over, the one named last changes fastest.
Arguments:
- tokens: float32 [1, 6144, 3072], P(None, 'seq', 'fsdp'), may hold values from -6 to 6
- block_mask: int32 [8, 6, 6], replicated, may hold values from 0 to 1, as said below
- space_qkv: bfloat16 [3072, 3, 512], P(None, None, 'fsdp'), may hold values from -0.109375 to 0.109375
- space_out: bfloat16 [512, 3072], P('fsdp'), may hold values from -0.375 to 0.375
- space_mod: float32 [3, 3072], replicated, may hold values from -2 to 3
- time_qkv: bfloat16 [3072, 3, 512], P(None, None, 'fsdp'), may hold values from -0.109375 to 0.109375
- time_out: bfloat16 [512, 3072], P('fsdp'), may hold values from -0.375 to 0.375
- time_mod: float32 [3, 3072], replicated, may hold values from -2 to 3
Outputs:
- result: float32 [1, 6144, 3072], P(None, 'seq', 'fsdp')
Inputs may be any that keep to these rules, and one draw needn't show every extreme that they name: block_mask[f, i, i] = 1 for every frame f and block i.
All inputs are finite; a program needn't handle non-finite values.
Results may differ from a plain program's by a relative error of at most 0.015.
Values may be sent and summed in bfloat16 or wider, within the bound.
A program may use at most 128 MiB of HBM per device.

v0:
```python
import math

import jax
import jax.numpy as jnp
from jax import lax
from jax.sharding import PartitionSpec as P

HD = 128
BLOCK = 128


EPS = 1e-06


def from_partner(shard, axis, distance):
    return lax.ppermute(shard, axis, [(i, i ^ 1 << distance) for i in range(lax.axis_size(axis))])


def modulate(stream, modulation):
    centre = jnp.mean(stream, axis=-1, keepdims=True)
    centred = stream - centre
    variance = jnp.mean(centred * centred, axis=-1, keepdims=True)
    normed = centred * lax.rsqrt(variance + EPS)
    return (normed * (1.0 + modulation[1]) + modulation[0]).astype(jnp.bfloat16)


def softmax_rounded(scores, reduce_axis):
    row_max = jnp.max(scores, axis=reduce_axis, keepdims=True)
    lifted = jnp.exp(scores - row_max)
    return (lifted / jnp.sum(lifted, axis=reduce_axis, keepdims=True)).astype(jnp.bfloat16)


def widen(shard):
    return lax.all_gather(shard, "fsdp", axis=2, tiled=True)


def head_total(partial_value):
    return lax.psum_scatter(
        partial_value.astype(jnp.bfloat16), "fsdp", scatter_dimension=2, tiled=True
    ).astype(jnp.float32)


def project_inputs(normed, qkv_weight):
    model_width = qkv_weight.shape[0]
    flat_rows = normed.reshape(-1, model_width)
    return jnp.dot(
        flat_rows, qkv_weight.reshape(model_width, -1), preferred_element_type=jnp.float32
    ).astype(jnp.bfloat16)


def on_device(tokens, block_mask, space_qkv, space_out, space_mod, time_qkv, time_out, time_mod):
    videos, row_count, part_width = tokens.shape
    model_width = space_qkv.shape[0]
    heads_width = space_qkv.shape[2]
    local_heads = heads_width // HD
    seq_count = lax.axis_size("seq")
    piece_rows = row_count // seq_count
    frame_count = seq_count // 2
    seq_index = lax.axis_index("seq")
    half_index = seq_index % 2
    frame_index = seq_index // 2
    feature_start = lax.axis_index("fsdp") * part_width
    score_scale = 1.0 / math.sqrt(HD)
    query_blocks = row_count // BLOCK
    key_blocks = 2 * query_blocks
    full_tokens = widen(tokens)
    packed = project_inputs(modulate(full_tokens, space_mod), space_qkv)
    packed = packed.reshape(videos, row_count, 3, local_heads, HD)
    queries = packed[:, :, 0]
    keys_values = packed[:, :, 1:]
    partner = from_partner(keys_values, "seq", 0)
    all_keys = jnp.where(
        half_index == 0,
        jnp.concatenate([keys_values, partner], axis=1),
        jnp.concatenate([partner, keys_values], axis=1),
    )
    zero_index = jnp.zeros((), jnp.int32)
    mask_rows = lax.dynamic_slice(
        block_mask,
        (frame_index, half_index * query_blocks, zero_index),
        (1, query_blocks, key_blocks),
    )[0]
    scores = (
        jnp.einsum(
            "bqhd,bkhd->bhqk", queries, all_keys[:, :, 0], preferred_element_type=jnp.float32
        )
        * score_scale
    )
    scores = scores.reshape(videos, local_heads, query_blocks, BLOCK, key_blocks, BLOCK)
    allowed = (mask_rows == 1)[None, None, :, None, :, None]
    scores = jnp.where(allowed, scores, -jnp.inf).reshape(
        videos, local_heads, row_count, 2 * row_count
    )
    weights_bf = softmax_rounded(scores, 3)
    attended = jnp.einsum(
        "bhqk,bkhd->bqhd", weights_bf, all_keys[:, :, 1], preferred_element_type=jnp.float32
    ).astype(jnp.bfloat16)
    partial_value = jnp.dot(
        attended.reshape(-1, heads_width), space_out, preferred_element_type=jnp.float32
    ).reshape(videos, row_count, model_width)
    summed = head_total(partial_value)
    space_gate = lax.dynamic_slice_in_dim(space_mod[2], feature_start, part_width, 0)
    stream = tokens + space_gate * summed
    wide_stream = widen(stream)
    packed_time = project_inputs(modulate(wide_stream, time_mod), time_qkv)
    arrived = lax.all_to_all(
        packed_time.reshape(videos, seq_count, piece_rows, 3 * heads_width),
        "seq",
        split_axis=1,
        concat_axis=1,
        tiled=True,
    )
    packed_time = arrived.reshape(videos, frame_count, 2 * piece_rows, 3, local_heads, HD)
    scores_time = (
        jnp.einsum(
            "bfphd,bgphd->bphfg",
            packed_time[:, :, :, 0],
            packed_time[:, :, :, 1],
            preferred_element_type=jnp.float32,
        )
        * score_scale
    )
    weights_time = softmax_rounded(scores_time, 4)
    attended_time = jnp.einsum(
        "bphfg,bgphd->bfphd",
        weights_time,
        packed_time[:, :, :, 2],
        preferred_element_type=jnp.float32,
    ).astype(jnp.bfloat16)
    returned = lax.all_to_all(
        attended_time.reshape(videos, seq_count, piece_rows, heads_width),
        "seq",
        split_axis=1,
        concat_axis=1,
        tiled=True,
    )
    partial_time = jnp.dot(
        returned.reshape(-1, heads_width), time_out, preferred_element_type=jnp.float32
    ).reshape(videos, row_count, model_width)
    summed_time = head_total(partial_time)
    time_gate = lax.dynamic_slice_in_dim(time_mod[2], feature_start, part_width, 0)
    return stream + time_gate * summed_time


def solution(mesh):
    placed = (
        P(None, "seq", "fsdp"),
        P(),
        P(None, None, "fsdp"),
        P("fsdp", None),
        P(),
        P(None, None, "fsdp"),
        P("fsdp", None),
        P(),
    )
    return jax.shard_map(
        on_device, mesh=mesh, in_specs=placed, out_specs=P(None, "seq", "fsdp"), check_vma=False
    )
```

profile of v0, /device:TPU:0, one launch (start us, length us, event | category | flops | bytes accessed | tf_op | source)
XLA Modules:
  0.0 293.6 jit_solution(683452697248010916)
XLA Ops:
  6.5 0.7 all-gather.3.cloned.1.call-update
  7.3 6.7 %copy.23 = bf16[3072,3,256]{0,2,1:T(8,128)(2,1)} copy(bf16[3072,3,256]{2,0,1:T(8,128)(2,1)} %param.10) | data formatting | bytes 9437184 | tf_op args[2]
  14.1 60.2 %all-gather.3.cloned.1.call-done = f32[1,384,3072]{2,1,0:T(8,128)} async-done(((f32[1,384,1536]{2,1,0:T(8,128)}), f32[1,384,3072]{2,1,0:T(8,128)}) %all-gather.3.cloned.1.call-update) | async-done | bytes 4718608 | tf_op jit(solution)/shard_map/all_gather | solution.py:34
  74.3 2.6 reduce_sum.54
  76.9 3.1 %multiply_reduce_fusion.1 = f32[384]{0:T(512)S(1)} fusion(f32[1,384,3072]{2,1,0:T(8,128)} %all-gather.3.cloned.1.call-done, f32[384]{0:T(512)S(1)} %broadcast_multiply_fusion.1), kind=kLoop, calls=%fused_computation.5 | loop fusion | flops 3538560 | bytes 4721664 | tf_op jit(solution)/shard_map/reduce_sum | solution.py:22
  80.0 0.7 copy-done.2
  80.7 4.7 %fusion.22 = bf16[384,768]{1,0:T(8,128)(2,1)S(1)} fusion(bf16[3072,768]{0,1:T(8,128)(2,1)} %bitcast.105, f32[1,384,3072]{2,1,0:T(8,128)S(1)} %copy-done.2, f32[3072]{0:T(1024)S(1)} %bitcast.115, f32[3072]{0:T(1024)S(1)} %bitcast.116, f32[384]{0:T(512)S(1)} %add_rsqrt_fusion.1, f32[384]{0:T(512)S(1)} %broadcast_multiply_fusion.1), kind=kOutput, calls=%fused_computation.29 | convolution fusion | flops 1818132480 | bytes 10054656 | tf_op jit(solution)/shard_map/dot_general | solution.py:46
  85.5 0.3 slice.52
  86.0 0.7 dynamic-slice_compare_fusion
  86.7 0.2 broadcast_in_dim.16
  86.9 0.9 copy.76
  87.9 1.3 maximum_select_fusion
  89.2 2.0 fusion.46
  91.3 2.9 fusion.31
  94.2 2.2 fusion.2
  96.5 34.9 %reduce-scatter.3.cloned.1.call-done = bf16[1,384,1536]{2,1,0:T(8,128)(2,1)} async-done(((bf16[1,384,3072]{2,1,0:T(8,128)(2,1)}), bf16[1,384,1536]{2,1,0:T(8,128)(2,1)}) %reduce-scatter.3.cloned.1.call-update) | async-done | bytes 1179664 | tf_op jit(solution)/shard_map/reduce_scatter | solution.py:38
  131.4 3.8 %multiply_add_fusion.1 = f32[1,384,1536]{2,1,0:T(8,128)} fusion(f32[1,384,1536]{2,1,0:T(8,128)} %param.8, bf16[1,384,1536]{2,1,0:T(8,128)(2,1)} %reduce-scatter.3.cloned.1.call-done, f32[1536]{0:T(1024)S(1)} %dynamic-slice_reduce_fusion.1), kind=kLoop, calls=%fused_computation.19 | loop fusion | flops 1769472 | bytes 5904384 | tf_op jit(solution)/shard_map/add | solution.py:103
  135.2 6.7 %copy.27 = bf16[3072,3,256]{0,2,1:T(8,128)(2,1)} copy(bf16[3072,3,256]{2,0,1:T(8,128)(2,1)} %param.13) | data formatting | bytes 9437184 | tf_op args[5]
  142.0 56.0 %all-gather.5.cloned.1.call-done = f32[1,384,3072]{2,1,0:T(8,128)} async-done(((f32[1,384,1536]{2,1,0:T(8,128)}), f32[1,384,3072]{2,1,0:T(8,128)}) %all-gather.5.cloned.1.call-update) | async-done | bytes 4718608 | tf_op jit(solution)/shard_map/all_gather | solution.py:34
  198.0 2.6 reduce_sum.57
  200.6 3.1 %multiply_reduce_fusion = f32[384]{0:T(512)S(1)} fusion(f32[1,384,3072]{2,1,0:T(8,128)} %all-gather.5.cloned.1.call-done, f32[384]{0:T(512)S(1)} %broadcast_multiply_fusion), kind=kLoop, calls=%fused_computation.3 | loop fusion | flops 3538560 | bytes 4721664 | tf_op jit(solution)/shard_map/reduce_sum | solution.py:22
  203.7 0.7 copy-done.1
  204.4 4.7 %fusion.19 = bf16[384,768]{1,0:T(8,128)(2,1)S(1)} fusion(bf16[3072,768]{0,1:T(8,128)(2,1)} %bitcast.104, f32[1,384,3072]{2,1,0:T(8,128)S(1)} %copy-done.1, f32[3072]{0:T(1024)S(1)} %bitcast.113, f32[3072]{0:T(1024)S(1)} %bitcast.114, f32[384]{0:T(512)S(1)} %add_rsqrt_fusion, f32[384]{0:T(512)S(1)} %broadcast_multiply_fusion), kind=kOutput, calls=%fused_computation.28 | convolution fusion | flops 1818132480 | bytes 10054656 | tf_op jit(solution)/shard_map/dot_general | solution.py:46
  209.1 22.7 %all_to_all.10 = bf16[1,16,24,768]{3,2,0,1:T(8,128)(2,1)S(1)} all-to-all(bf16[1,16,24,768]{3,2,0,1:T(8,128)(2,1)S(1)} %bitcast.109), channel_id=1, replica_groups=mesh['seq'=16,'fsdp'=2] {'seq'}, dimensions={1} | all-to-all | bytes 1179648 | tf_op jit(solution)/shard_map/all_to_all | solution.py:106
  231.9 1.1 fusion.43
  233.0 2.8 fusion.47
  235.8 1.3 fusion.32
  237.1 0.2 copy.33
  237.4 11.8 %all_to_all.11 = bf16[1,16,24,256]{3,2,0,1:T(8,128)(2,1)S(1)} all-to-all(bf16[1,16,24,256]{3,2,0,1:T(8,128)(2,1)S(1)} %bitcast.108), channel_id=1, replica_groups=mesh['seq'=16,'fsdp'=2] {'seq'}, dimensions={1} | all-to-all | bytes 393216 | tf_op jit(solution)/shard_map/all_to_all | solution.py:130
  249.2 2.2 fusion.3
  251.5 31.9 %reduce-scatter.5.cloned.1.call-done = bf16[1,384,1536]{2,1,0:T(8,128)(2,1)} async-done(((bf16[1,384,3072]{2,1,0:T(8,128)(2,1)}), bf16[1,384,1536]{2,1,0:T(8,128)(2,1)}) %reduce-scatter.5.cloned.1.call-update) | async-done | bytes 1179664 | tf_op jit(solution)/shard_map/reduce_scatter | solution.py:38
  283.3 3.8 %multiply_add_fusion = f32[1,384,1536]{2,1,0:T(8,128)} fusion(f32[1,384,1536]{2,1,0:T(8,128)} %multiply_add_fusion.1, bf16[1,384,1536]{2,1,0:T(8,128)(2,1)} %reduce-scatter.5.cloned.1.call-done, f32[1536]{0:T(1024)S(1)} %dynamic-slice_reduce_fusion), kind=kLoop, calls=%fused_computation.14 | loop fusion | flops 1769472 | bytes 5904384 | tf_op jit(solution)/shard_map/add | solution.py:142
  (33 shorter events, 1.0 us)
Async XLA Ops:
  6.5 87.6 %copy-start = (bf16[256,3072]{1,0:T(8,128)(2,1)S(1)}, bf16[256,3072]{1,0:T(8,128)(2,1)}, u32[]{:S(2)}) copy-start(bf16[256,3072]{1,0:T(8,128)(2,1)} %param.11) | copy-start | bytes 4718596
  6.5 67.8 %all-gather.3.cloned.1.call-start = ((), (), s32[]{:S(2)}) async-start(), calls=%async_computation.4 | async-start | bytes 7077888 | tf_op jit(solution)/shard_map/all_gather | solution.py:34
  7.3 6.8 %copy-start.4 = (f32[3,3072]{1,0:T(4,128)S(1)}, f32[3,3072]{1,0:T(4,128)}, u32[]{:S(2)}) copy-start(f32[3,3072]{1,0:T(4,128)} %param.12) | copy-start | bytes 110596
  7.3 124.1 %reduce-scatter.3.cloned.1.call-start = ((), (), s32[]{:S(2)}) async-start(), calls=%async_computation.5 | async-start | bytes 3538944 | tf_op jit(solution)/shard_map/reduce_scatter | solution.py:38
  76.9 3.8 %copy-start.2 = (f32[1,384,3072]{2,1,0:T(8,128)S(1)}, f32[1,384,3072]{2,1,0:T(8,128)}, u32[]{:S(2)}) copy-start(f32[1,384,3072]{2,1,0:T(8,128)} %all-gather.3.cloned.1.call-done) | copy-start | bytes 14155780
  85.8 2.0 collective-permute-start
  96.4 101.6 %all-gather.5.cloned.1.call-start = ((), (), s32[]{:S(2)}) async-start(), calls=%async_computation.6 | async-start | bytes 7077888 | tf_op jit(solution)/shard_map/all_gather | solution.py:34
  135.2 6.8 %copy-start.5 = (f32[3,3072]{1,0:T(4,128)S(1)}, f32[3,3072]{1,0:T(4,128)}, u32[]{:S(2)}) copy-start(f32[3,3072]{1,0:T(4,128)} %param.15) | copy-start | bytes 110596
  135.2 148.2 %reduce-scatter.5.cloned.1.call-start = ((), (), s32[]{:S(2)}) async-start(), calls=%async_computation.7 | async-start | bytes 3538944 | tf_op jit(solution)/shard_map/reduce_scatter | solution.py:38
  200.6 3.8 %copy-start.1 = (f32[1,384,3072]{2,1,0:T(8,128)S(1)}, f32[1,384,3072]{2,1,0:T(8,128)}, u32[]{:S(2)}) copy-start(f32[1,384,3072]{2,1,0:T(8,128)} %all-gather.5.cloned.1.call-done) | copy-start | bytes 14155780
  233.0 16.2 %copy-start.3 = (bf16[256,3072]{1,0:T(8,128)(2,1)S(1)}, bf16[256,3072]{1,0:T(8,128)(2,1)}, u32[]{:S(2)}) copy-start(bf16[256,3072]{1,0:T(8,128)(2,1)} %param.14) | copy-start | bytes 4718596
Sparse Core Ops, SparseCore 0:
  8.9 65.3 all-gather.2
  96.5 34.8 reduce-scatter.2
  135.3 62.6 all-gather.4
  251.5 31.7 reduce-scatter.4
where the time goes:
time: 294 us
  waiting for transfers between devices  184 us (63%)
  blocking collectives  34.5 us (12%)
  matrix products  22.8 us (8%)
  other arithmetic  21.1 us (7%)
  local copies, waits for them, and re-layouts  17.9 us (6%)
  between operations  13.3 us (5%)
    all_gather x2, waiting for transfers between devices, widen(): return lax.all_gather(shard, 'fsdp', axis=2, tiled=True)  116 us
    reduce_scatter x2, waiting for transfers between devices, head_total(): lax.psum_scatter(partial_value.astype(jnp.bfloat16), 'fsdp', scatter_dime...  66.8 us
    all_to_all x1, blocking collectives, on_device(): lax.all_to_all(packed_time.reshape(videos, seq_count, piece_rows, 3 * hea...  22.7 us
    unnamed x17, local copies, waits for them, and re-layouts  15.7 us
    all_to_all x1, blocking collectives, on_device(): lax.all_to_all(attended_time.reshape(videos, seq_count, piece_rows, heads...  11.8 us
    dot_general x2, matrix products, project_inputs(): jnp.dot(flat_rows, qkv_weight.reshape(model_width, -1), preferred_element...  9.34 us
    reduce_sum x2, other arithmetic, modulate(): variance = jnp.mean(centred * centred, axis=-1, keepdims=True)  6.18 us
  transfers between devices with their start and end apart: 5, of which 4 were waited for; matrix products, arithmetic and copies ran while one was open for 5% of the time, Pallas kernels for 0%

commit v1 on v0

v1 whole, which is shorter than its diff:
```python
import functools
import math

import jax
import jax.numpy as jnp
from jax import lax
from jax.experimental import pallas as pl
from jax.experimental.pallas import tpu as pltpu
from jax.sharding import PartitionSpec as P

HD = 128
BLOCK = 128
EPS = 1e-06
GROUP = 4
MESH = pl.DeviceIdType.MESH
NT = (((1,), (1,)), ((), ()))


def softmax_rounded(scores):
    row_max = jnp.max(scores, axis=1, keepdims=True)
    lifted = jnp.exp(scores - row_max)
    return (lifted / jnp.sum(lifted, axis=1, keepdims=True)).astype(jnp.bfloat16)


def sublayers(
    sizes,
    mask_ref, tokens_ref, space_qkv_ref, space_out_ref, space_mod_ref, time_qkv_ref, time_out_ref,
    time_mod_ref, result_ref,
    stream, cols, total, queries, keys_values, mixed, sent_qkv, got_qkv, sent_att,
    qkv_w, out_w, mods, stats, normed, att_space, att_time,
    in_sem, w_sem, o_sem, m_sem, out_sem,
    stat_s, stat_r, h_s, h_r, kv_s, kv_r, as_s, as_r, at_s, at_r, wq_s, wq_r, wf_s, wf_r,
    tq_s, tq_r, ta_s, ta_r,
):
    frames, parts, rows, part_width, heads_width, chunk = sizes
    chunks = rows // chunk
    piece = rows // frames
    per_chunk = chunk // piece
    query_blocks = rows // BLOCK
    local_heads = heads_width // HD
    width = part_width * parts
    quarter = heads_width // GROUP
    scale = 1.0 / math.sqrt(HD)

    seq = lax.axis_index("seq")
    me = lax.axis_index("fsdp")
    half = lax.rem(seq, 2)
    frame = seq // 2
    member = lax.rem(seq, GROUP)
    group = seq - member

    def peer(distance):
        return lax.rem(me + distance, parts)

    def source(distance):
        return lax.rem(me + parts - distance, parts)

    def fsdp_copy(src, dst, send, recv, distance):
        return pltpu.make_async_remote_copy(
            src_ref=src, dst_ref=dst, send_sem=send, recv_sem=recv,
            device_id={"fsdp": peer(distance)}, device_id_type=MESH,
        )

    def seq_copy(src, dst, send, recv, target):
        return pltpu.make_async_remote_copy(
            src_ref=src, dst_ref=dst, send_sem=send, recv_sem=recv,
            device_id={"seq": target}, device_id_type=MESH,
        )

    qkv_refs = (space_qkv_ref, time_qkv_ref)
    out_refs = (space_out_ref, time_out_ref)
    mod_refs = (space_mod_ref, time_mod_ref)
    own_columns = pl.ds(pl.multiple_of(me * part_width, 128), part_width)

    def load_tokens():
        return pltpu.make_async_copy(tokens_ref.at[0], stream, in_sem)

    def load_qkv(layer):
        return pltpu.make_async_copy(qkv_refs[layer], qkv_w.at[layer], w_sem.at[layer])

    def load_out(layer):
        return pltpu.make_async_copy(
            out_refs[layer].at[:, own_columns], out_w.at[layer, me], o_sem.at[layer]
        )

    def load_mod(layer):
        return pltpu.make_async_copy(
            mod_refs[layer].at[:, own_columns], mods.at[layer], m_sem.at[layer]
        )

    load_tokens().start()
    for layer in range(2):
        load_mod(layer).start()
    load_qkv(0).start()
    load_out(0).start()

    barrier = pltpu.get_barrier_semaphore()
    for distance in range(1, parts):
        pl.semaphore_signal(barrier, inc=1, device_id={"fsdp": peer(distance)}, device_id_type=MESH)
    for distance in range(1, frames):
        other = lax.rem(frame + distance, frames) * 2 + half
        pl.semaphore_signal(barrier, inc=1, device_id={"seq": other}, device_id_type=MESH)
    for distance in range(GROUP // 2):
        other = group + lax.rem(member + 1 + 2 * distance, GROUP)
        pl.semaphore_signal(barrier, inc=1, device_id={"seq": other}, device_id_type=MESH)
    pl.semaphore_wait(barrier, parts - 1 + frames - 1 + GROUP // 2)

    own_quarter = pl.ds(pl.multiple_of(member * quarter, 16), quarter)

    def weight_copy(layer, distance):
        target = peer(distance)
        columns = pl.ds(pl.multiple_of(target * part_width, 128), part_width)
        return fsdp_copy(
            out_refs[layer].at[own_quarter, columns], out_w.at[layer, me, own_quarter],
            wq_s.at[layer, distance], wq_r.at[layer, distance], distance,
        )

    def spread_copy(layer, distance, step):
        block = out_w.at[layer, source(distance), own_quarter]
        return seq_copy(
            block, block, wf_s.at[layer, distance, step], wf_r.at[layer, distance, step],
            group + lax.rem(member + step, GROUP),
        )

    def arrived_spread(layer, distance, step):
        first = lax.rem(member + GROUP - step, GROUP) * quarter
        block = out_w.at[layer, source(distance), pl.ds(pl.multiple_of(first, 16), quarter)]
        return seq_copy(
            block, block, wf_s.at[layer, distance, step], wf_r.at[layer, distance, step],
            group + lax.rem(member + step, GROUP),
        )

    def send_weights(layer):
        for distance in range(1, parts):
            weight_copy(layer, distance).start()

    def spread_weights(layer):
        for distance in range(1, parts):
            weight_copy(layer, distance).wait_recv()
            for step in range(1, GROUP):
                spread_copy(layer, distance, step).start()

    def finish_weights(layer):
        load_out(layer).wait()
        for distance in range(1, parts):
            for step in range(1, GROUP):
                arrived_spread(layer, distance, step).wait_recv()

    def note_statistics(values, start, count):
        centre = jnp.sum(values, axis=1, keepdims=True) * (1.0 / part_width)
        offset = values - centre
        spread = jnp.sum(offset * offset, axis=1, keepdims=True)
        lane = lax.broadcasted_iota(jnp.int32, (count, 128), 1)
        cols[pl.ds(start, count), :] = jnp.where(lane == 0, centre, spread)

    def stat_copy(layer, distance):
        return fsdp_copy(
            stats.at[layer, me], stats.at[layer, me],
            stat_s.at[layer, distance], stat_r.at[layer, distance], distance,
        )

    def send_statistics(layer):
        stats[layer, me] = jnp.transpose(cols[...])[:8]
        for distance in range(1, parts):
            stat_copy(layer, distance).start()

    def finish_statistics(layer):
        for distance in range(1, parts):
            stat_copy(layer, distance).wait_recv()
        centre = jnp.zeros((1, rows), jnp.float32)
        for part in range(parts):
            centre = centre + stats[layer, part][0:1]
        centre = centre * (1.0 / parts)
        spread = jnp.zeros((1, rows), jnp.float32)
        for part in range(parts):
            shift = stats[layer, part][0:1] - centre
            spread = spread + stats[layer, part][1:2] * (1.0 / part_width) + shift * shift
        inverse = lax.rsqrt(spread * (1.0 / parts) + EPS)
        line = lax.broadcasted_iota(jnp.int32, (128, rows), 0)
        cols[...] = jnp.transpose(jnp.where(line == 0, centre, inverse))

    def chunk_rows(index):
        return pl.ds(pl.multiple_of(index * chunk, chunk), chunk)

    def block_rows(index):
        return pl.ds(pl.multiple_of(index * BLOCK, BLOCK), BLOCK)

    def h_copy(layer, index, distance):
        block = normed.at[layer, me, chunk_rows(index)]
        return fsdp_copy(
            block, block, h_s.at[layer, distance, index], h_r.at[layer, distance, index], distance
        )

    def send_normed(layer, order):
        shift = mods[layer, 0:1]
        gain = 1.0 + mods[layer, 1:2]

        def step(i, carry):
            index = order(i)
            span = chunk_rows(index)
            values = stream[span, :]
            line = cols[span, :]
            out = (values - line[:, 0:1]) * line[:, 1:2] * gain + shift
            normed[layer, me, span, :] = out.astype(jnp.bfloat16)
            for distance in range(1, parts):
                h_copy(layer, index, distance).start()
            return carry

        lax.fori_loop(0, chunks, step, 0)

    def own_product(layer):
        depth = pl.ds(pl.multiple_of(me * part_width, 128), part_width)

        def step(index, carry):
            span = block_rows(index)
            total[span, :] = jnp.dot(
                normed[layer, me, span, :], qkv_w[layer, depth, :],
                preferred_element_type=jnp.float32,
            )
            return carry

        lax.fori_loop(0, query_blocks, step, 0)

    def chunk_product(layer, index):
        span = chunk_rows(index)
        value = total[span, :]
        for distance in range(1, parts):
            other = source(distance)
            depth = pl.ds(pl.multiple_of(other * part_width, 128), part_width)
            value = value + jnp.dot(
                normed[layer, other, span, :], qkv_w[layer, depth, :],
                preferred_element_type=jnp.float32,
            )
        return value

    def wait_chunk(layer, index):
        for distance in range(1, parts):
            h_copy(layer, index, distance).wait_recv()

    load_tokens().wait()

    def first_statistics(i, carry):
        start = pl.multiple_of(i * chunk, chunk)
        note_statistics(stream[pl.ds(start, chunk), :], start, chunk)
        return carry

    lax.fori_loop(0, chunks, first_statistics, 0)
    send_statistics(0)
    send_weights(0)
    for layer in range(2):
        load_mod(layer).wait()
    load_qkv(1).start()
    load_out(1).start()
    finish_statistics(0)
    send_normed(0, lambda i: i)
    send_weights(1)
    load_qkv(0).wait()
    own_product(0)
    spread_weights(0)

    def kv_copy(index):
        block = keys_values.at[half, :, chunk_rows(index)]
        return seq_copy(block, block, kv_s.at[index], kv_r.at[index], seq + 1 - 2 * half)

    def space_chunk(index, carry):
        wait_chunk(0, index)
        span = chunk_rows(index)
        value = chunk_product(0, index).astype(jnp.bfloat16)
        queries[span, :] = value[:, :heads_width]
        for kind in range(2):
            first = (kind + 1) * heads_width
            keys_values[half, kind, span, :] = value[:, first:first + heads_width]
        kv_copy(index).start()
        return carry

    lax.fori_loop(0, chunks, space_chunk, 0)
    spread_weights(1)

    def wait_keys(index, carry):
        kv_copy(index).wait_recv()
        return carry

    lax.fori_loop(0, chunks, wait_keys, 0)

    def att_space_copy(index, distance):
        block = att_space.at[me, block_rows(index)]
        return fsdp_copy(
            block, block, as_s.at[distance, index], as_r.at[distance, index], distance
        )

    def space_attention(index, carry):
        span = block_rows(index)
        bias = []
        for key_block in range(2 * query_blocks):
            kept = mask_ref[frame, half * query_blocks + index, key_block]
            bias.append(jnp.full((1, BLOCK), jnp.where(kept == 1, 0.0, -jnp.inf), jnp.float32))
        bias = jnp.concatenate(bias, axis=1)
        for head in range(local_heads):
            lanes = slice(head * HD, (head + 1) * HD)
            keys = keys_values[:, 0, :, lanes].reshape(2 * rows, HD)
            values = keys_values[:, 1, :, lanes].reshape(2 * rows, HD)
            scores = lax.dot_general(
                queries[span, lanes], keys, NT, preferred_element_type=jnp.float32
            )
            weights = softmax_rounded(scores * scale + bias)
            att_space[me, span, lanes] = jnp.dot(
                weights, values, preferred_element_type=jnp.float32
            ).astype(jnp.bfloat16)
        for distance in range(1, parts):
            att_space_copy(index, distance).start()
        return carry

    lax.fori_loop(0, query_blocks, space_attention, 0)
    finish_weights(0)

    def space_project(index, carry):
        span = block_rows(index)
        for distance in range(1, parts):
            att_space_copy(index, distance).wait_recv()
        summed = jnp.zeros((BLOCK, part_width), jnp.float32)
        for part in range(parts):
            summed = summed + jnp.dot(
                att_space[part, span, :], out_w[0, part], preferred_element_type=jnp.float32
            ).astype(jnp.bfloat16).astype(jnp.float32)
        values = stream[span, :] + mods[0, 2:3] * summed
        stream[span, :] = values
        note_statistics(values, pl.multiple_of(index * BLOCK, BLOCK), BLOCK)
        return carry

    lax.fori_loop(0, query_blocks, space_project, 0)

    send_statistics(1)
    load_qkv(1).wait()
    finish_statistics(1)

    def time_order(i):
        return lax.rem(frame // per_chunk + 1 + i, chunks)

    send_normed(1, time_order)
    own_product(1)

    def tq_copy(target):
        return seq_copy(
            sent_qkv.at[target], got_qkv.at[frame], tq_s.at[target], tq_r.at[frame],
            target * 2 + half,
        )

    def tq_arrival(origin):
        return seq_copy(
            sent_qkv.at[origin], got_qkv.at[origin], tq_s.at[origin], tq_r.at[origin],
            origin * 2 + half,
        )

    def time_chunk(i, carry):
        index = time_order(i)
        wait_chunk(1, index)
        whole = chunk_product(1, index).reshape(per_chunk, piece, 3 * heads_width)
        whole = whole.astype(jnp.bfloat16)
        for n in range(per_chunk):
            target = index * per_chunk + n
            sent_qkv[target] = whole[n]

            @pl.when(target != frame)
            def _():
                tq_copy(target).start()

        return carry

    lax.fori_loop(0, chunks, time_chunk, 0)
    got_qkv[frame] = sent_qkv[frame]

    def others(action):
        def step(i, carry):
            action(lax.rem(frame + frames - 1 - i, frames))
            return carry

        lax.fori_loop(0, frames - 1, step, 0)

    others(lambda origin: tq_arrival(origin).wait_recv())

    def position(index):
        passed = jnp.zeros_like(index)
        for n in range(1, frames):
            passed = passed + jnp.where(index >= n * piece, piece, 0)
        return index - passed

    def flat(first):
        return got_qkv[:, :, first:first + HD].astype(jnp.float32).reshape(rows, HD).astype(jnp.bfloat16)

    column = position(lax.broadcasted_iota(jnp.int32, (1, rows), 1))
    for head in range(local_heads):
        first = head * HD
        head_queries = flat(first)
        head_keys = flat(heads_width + first)
        head_values = flat(2 * heads_width + first)
        for block in range(query_blocks):
            span = slice(block * BLOCK, (block + 1) * BLOCK)
            line = position(lax.broadcasted_iota(jnp.int32, (BLOCK, 1), 0) + block * BLOCK)
            scores = lax.dot_general(
                head_queries[span], head_keys, NT, preferred_element_type=jnp.float32
            ) * scale
            weights = softmax_rounded(jnp.where(line == column, scores, -jnp.inf))
            mixed[span, first:first + HD] = jnp.dot(
                weights, head_values, preferred_element_type=jnp.float32
            )
    sent_att[...] = mixed[...].reshape(frames, piece, heads_width).astype(jnp.bfloat16)
    att_time[me, frame] = sent_att[frame]

    def ta_copy(target):
        return seq_copy(
            sent_att.at[target], att_time.at[me, frame], ta_s.at[target], ta_r.at[frame],
            target * 2 + half,
        )

    def ta_arrival(origin):
        return seq_copy(
            sent_att.at[origin], att_time.at[me, origin], ta_s.at[origin], ta_r.at[origin],
            origin * 2 + half,
        )

    def send_att(i, carry):
        ta_copy(lax.rem(frame + 1 + i, frames)).start()
        return carry

    lax.fori_loop(0, frames - 1, send_att, 0)

    def att_time_copy(index, distance):
        block = att_time.at[me, index]
        return fsdp_copy(
            block, block, at_s.at[distance, index], at_r.at[distance, index], distance
        )

    def forward(index):
        for distance in range(1, parts):
            att_time_copy(index, distance).start()

    forward(frame)

    def relay(origin):
        ta_arrival(origin).wait_recv()
        forward(origin)

    others(relay)
    finish_weights(1)

    def result_copy(index):
        span = chunk_rows(index)
        return pltpu.make_async_copy(stream.at[span], result_ref.at[0, span], out_sem.at[index])

    def time_project(i, carry):
        index = lax.rem(frame // per_chunk + chunks - i, chunks)
        span = chunk_rows(index)
        for n in range(per_chunk):
            for distance in range(1, parts):
                att_time_copy(index * per_chunk + n, distance).wait_recv()
        summed = jnp.zeros((chunk, part_width), jnp.float32)
        for part in range(parts):
            attended = att_time[part, pl.ds(index * per_chunk, per_chunk)].astype(jnp.float32)
            summed = summed + jnp.dot(
                attended.reshape(chunk, heads_width).astype(jnp.bfloat16), out_w[1, part],
                preferred_element_type=jnp.float32,
            ).astype(jnp.bfloat16).astype(jnp.float32)
        stream[span, :] = stream[span, :] + mods[1, 2:3] * summed
        result_copy(index).start()
        return carry

    lax.fori_loop(0, chunks, time_project, 0)

    def drain(i, carry):
        kv_copy(i).wait_send()
        for layer in range(2):
            for distance in range(1, parts):
                h_copy(layer, i, distance).wait_send()
        result_copy(i).wait()
        return carry

    lax.fori_loop(0, chunks, drain, 0)

    def drain_blocks(i, carry):
        for distance in range(1, parts):
            att_space_copy(i, distance).wait_send()
        return carry

    lax.fori_loop(0, query_blocks, drain_blocks, 0)

    def drain_pieces(i, carry):
        for distance in range(1, parts):
            att_time_copy(i, distance).wait_send()
        return carry

    lax.fori_loop(0, frames, drain_pieces, 0)

    def drain_other(target):
        tq_copy(target).wait_send()
        ta_copy(target).wait_send()

    others(drain_other)
    for layer in range(2):
        for distance in range(1, parts):
            stat_copy(layer, distance).wait_send()
            weight_copy(layer, distance).wait_send()
            for step in range(1, GROUP):
                spread_copy(layer, distance, step).wait_send()


def on_device(tokens, block_mask, space_qkv, space_out, space_mod, time_qkv, time_out, time_mod):
    videos, rows, part_width = tokens.shape
    heads_width = space_qkv.shape[2]
    frames = lax.axis_size("seq") // 2
    parts = lax.axis_size("fsdp")
    piece = rows // frames
    chunk = piece if piece % 16 == 0 else 2 * piece
    chunks = rows // chunk
    blocks = rows // BLOCK
    width = part_width * parts
    bf16, f32 = jnp.bfloat16, jnp.float32
    dma = pltpu.SemaphoreType.DMA
    hbm = pl.BlockSpec(memory_space=pl.ANY)
    scratch = [
        pltpu.VMEM((rows, part_width), f32),
        pltpu.VMEM((rows, 128), f32),
        pltpu.VMEM((rows, 3 * heads_width), f32),
        pltpu.VMEM((rows, heads_width), bf16),
        pltpu.VMEM((2, 2, rows, heads_width), bf16),
        pltpu.VMEM((rows, heads_width), f32),
        pltpu.VMEM((frames, piece, 3 * heads_width), bf16),
        pltpu.VMEM((frames, piece, 3 * heads_width), bf16),
        pltpu.VMEM((frames, piece, heads_width), bf16),
        pltpu.VMEM((2, width, 3 * heads_width), bf16),
        pltpu.VMEM((2, parts, heads_width, part_width), bf16),
        pltpu.VMEM((2, 3, part_width), f32),
        pltpu.VMEM((2, parts, 8, rows), f32),
        pltpu.VMEM((2, parts, rows, part_width), bf16),
        pltpu.VMEM((parts, rows, heads_width), bf16),
        pltpu.VMEM((parts, frames, piece, heads_width), bf16),
        dma, dma((2,)), dma((2,)), dma((2,)), dma((chunks,)),
        dma((2, parts)), dma((2, parts)),
        dma((2, parts, chunks)), dma((2, parts, chunks)),
        dma((chunks,)), dma((chunks,)),
        dma((parts, blocks)), dma((parts, blocks)),
        dma((parts, frames)), dma((parts, frames)),
        dma((2, parts)), dma((2, parts)),
        dma((2, parts, GROUP)), dma((2, parts, GROUP)),
        dma((frames,)), dma((frames,)),
        dma((frames,)), dma((frames,)),
    ]
    sizes = (frames, parts, rows, part_width, heads_width, chunk)
    return pl.pallas_call(
        functools.partial(sublayers, sizes),
        out_shape=jax.ShapeDtypeStruct(tokens.shape, f32),
        in_specs=[pl.BlockSpec(memory_space=pltpu.SMEM)] + [hbm] * 7,
        out_specs=hbm,
        scratch_shapes=scratch,
        compiler_params=pltpu.CompilerParams(
            collective_id=0, has_side_effects=True, vmem_limit_bytes=52 * 1024 * 1024
        ),
        cost_estimate=pl.CostEstimate(
            flops=4 * rows * width * 4 * heads_width, bytes_accessed=20 * 1024 * 1024,
            transcendentals=1024 * 1024,
        ),
    )(
        block_mask, tokens, space_qkv.reshape(width, -1), space_out, space_mod,
        time_qkv.reshape(width, -1), time_out, time_mod,
    )


def solution(mesh):
    placed = (
        P(None, "seq", "fsdp"),
        P(),
        P(None, None, "fsdp"),
        P("fsdp", None),
        P(),
        P(None, None, "fsdp"),
        P("fsdp", None),
        P(),
    )
    return jax.shard_map(
        on_device, mesh=mesh, in_specs=placed, out_specs=P(None, "seq", "fsdp"), check_vma=False
    )
```

time: 294 us -> 130 us (0.44)
  waiting for transfers between devices: 184 us -> 0 us
  Pallas kernels: 0 us -> 98.9 us
  blocking collectives: 34.5 us -> 0 us
  matrix products: 22.8 us -> 0 us
  other arithmetic: 21.1 us -> 0 us
  between operations: 13.3 us -> 0.05 us
  local copies, waits for them, and re-layouts: 17.9 us -> 30 us
    all_gather x2 -> x0, waiting for transfers between devices: 116 us -> none  [widen(): return lax.all_gather(shard, 'fsdp', axis=2, tiled=True)]
    pallas_call x0 -> x1, Pallas kernels: none -> 98.9 us  [on_device(): pl.pallas_call(functools.partial(sublayers, sizes), out_shape=jax.ShapeDt...]
    reduce_scatter x2 -> x0, waiting for transfers between devices: 66.8 us -> none  [head_total(): lax.psum_scatter(partial_value.astype(jnp.bfloat16), 'fsdp', scatter_dime...]
    all_to_all x2 -> x0, blocking collectives: 34.5 us -> none  [the longest x1 22.7 us: on_device(): lax.all_to_all(packed_time.reshape(videos, seq_count, piece_rows, 3 * hea...]
    dot_general x6 -> x0, matrix products: 18 us -> none  [the longest x2 9.34 us: project_inputs(): jnp.dot(flat_rows, qkv_weight.reshape(model_width, -1), preferred_element...]
    reshape x3 -> x2, local copies, waits for them, and re-layouts: 0.4 us -> 13.5 us  [the longest x1 6.82 us: on_device(): time_qkv.reshape(width, -1)]
    reduce_sum x4 -> x0, other arithmetic: 11.4 us -> none  [the longest x2 6.18 us: modulate(): variance = jnp.mean(centred * centred, axis=-1, keepdims=True)]
    add x2 -> x0, other arithmetic: 7.51 us -> none  [the longest x1 3.76 us: on_device(): stream = tokens + space_gate * summed]
  transfers between devices with their start and end apart: 5 -> 0, of which waited for: 4 -> 0; matrix products, arithmetic and copies ran while one was open for 5% -> 0% of each run, Pallas kernels for 0% -> 0%
where the time goes in v1:
time: 130 us; the launch traced here: 129 us
  Pallas kernels  98.9 us (76%)
  local copies, waits for them, and re-layouts  30 us (23%)
    pallas_call x1, Pallas kernels, on_device(): pl.pallas_call(functools.partial(sublayers, sizes), out_shape=jax.ShapeDt...  98.9 us
    unnamed x12, local copies, waits for them, and re-layouts  16.5 us
    reshape x1, local copies, waits for them, and re-layouts, on_device(): time_qkv.reshape(width, -1)  6.82 us
    reshape x1, local copies, waits for them, and re-layouts, on_device(): space_qkv.reshape(width, -1)  6.64 us

profile of v1, /device:TPU:0, one launch (start us, length us, event | category | flops | bytes accessed | tf_op | source)
XLA Modules:
  0.0 129.0 jit_solution(12669979026895549640)
XLA Ops:
  0.0 6.7 %copy.12 = bf16[3072,3,256]{0,2,1:T(8,128)(2,1)} copy(bf16[3072,3,256]{2,0,1:T(8,128)(2,1)} %param.10) | data formatting | bytes 9437184 | tf_op args[2]
  6.7 6.6 %copy.15.space_qkv_ref = bf16[3072,768]{1,0:T(8,128)(2,1)} copy(bf16[3072,768]{0,1:T(8,128)(2,1)} %bitcast.2) | data formatting | bytes 9437184 | tf_op jit(solution)/shard_map/reshape | solution.py:562
  13.3 6.6 %copy.13 = bf16[3072,3,256]{0,2,1:T(8,128)(2,1)} copy(bf16[3072,3,256]{2,0,1:T(8,128)(2,1)} %param.13) | data formatting | bytes 9437184 | tf_op args[5]
  19.9 0.0 copy-start.3
  19.9 0.0 copy-start
  19.9 0.0 copy-start.1
  20.0 0.0 copy-start.2
  20.0 6.8 %copy.16.time_qkv_ref = bf16[3072,768]{1,0:T(8,128)(2,1)} copy(bf16[3072,768]{0,1:T(8,128)(2,1)} %bitcast.3) | data formatting | bytes 9437184 | tf_op jit(solution)/shard_map/reshape | solution.py:563
  26.8 0.0 copy-done.3
  26.8 0.0 copy-done
  26.8 0.0 copy-done.1
  26.8 0.0 copy-done.2
  26.8 98.9 %shard_map.82 = f32[1,384,1536]{2,1,0:T(8,128)} custom-call(s32[8,6,6]{2,1,0:T(8,128)S(1)} %copy.14.mask_ref, f32[1,384,1536]{2,1,0:T(8,128)} %tokens_ref.1, bf16[3072,768]{1,0:T(8,128)(2,1)} %copy.15.space_qkv_ref, bf16[256,3072]{1,0:T(8,128)(2,1)S(1)} %copy-done, f32[3,3072]{1,0:T(4,128)S(1)} %copy-done.1, bf16[3072,768]{1,0:T(8,128)(2,1)} %copy.16.time_qkv_ref, ...), custom_call_target="tpu_custom_call" | custom-call | flops 4831838208 | bytes 20971520 | tf_op jit(solution)/shard_map/pallas_call | solution.py:548
  125.7 3.2 %copy.18 = f32[1,384,1536]{2,1,0:T(8,128)} copy(f32[1,384,1536]{2,1,0:T(8,128)} %shard_map.82) | data formatting | bytes 4718592
  (1 shorter events, 0.0 us)
Async XLA Ops:
  19.9 6.8 %copy-start.3 = (s32[8,6,6]{2,0,1:T(8,128)S(1)}, s32[8,6,6]{2,0,1:T(8,128)}, u32[]{:S(2)}) copy-start(s32[8,6,6]{2,0,1:T(8,128)} %param.9) | copy-start | bytes 3460
  19.9 6.8 %copy-start = (bf16[256,3072]{1,0:T(8,128)(2,1)S(1)}, bf16[256,3072]{1,0:T(8,128)(2,1)}, u32[]{:S(2)}) copy-start(bf16[256,3072]{1,0:T(8,128)(2,1)} %space_out_ref.1) | copy-start | bytes 4718596
  19.9 6.9 %copy-start.1 = (f32[3,3072]{1,0:T(4,128)S(1)}, f32[3,3072]{1,0:T(4,128)}, u32[]{:S(2)}) copy-start(f32[3,3072]{1,0:T(4,128)} %space_mod_ref.1) | copy-start | bytes 110596
  20.0 6.9 %copy-start.2 = (f32[3,3072]{1,0:T(4,128)S(1)}, f32[3,3072]{1,0:T(4,128)}, u32[]{:S(2)}) copy-start(f32[3,3072]{1,0:T(4,128)} %time_mod_ref.1) | copy-start | bytes 110596

commit v2 on v1

--- a/solution.py
+++ b/solution.py
@@ -75,8 +75,11 @@
     def load_tokens():
         return pltpu.make_async_copy(tokens_ref.at[0], stream, in_sem)
 
-    def load_qkv(layer):
-        return pltpu.make_async_copy(qkv_refs[layer], qkv_w.at[layer], w_sem.at[layer])
+    def load_qkv(layer, kind):
+        lanes = pl.ds(kind * heads_width, heads_width)
+        return pltpu.make_async_copy(
+            qkv_refs[layer].at[kind], qkv_w.at[layer, :, lanes], w_sem.at[layer, kind]
+        )
 
     def load_out(layer):
         return pltpu.make_async_copy(
@@ -91,7 +94,8 @@
     load_tokens().start()
     for layer in range(2):
         load_mod(layer).start()
-    load_qkv(0).start()
+    for kind in range(3):
+        load_qkv(0, kind).start()
     load_out(0).start()
 
     barrier = pltpu.get_barrier_semaphore()
@@ -249,12 +253,14 @@
     send_weights(0)
     for layer in range(2):
         load_mod(layer).wait()
-    load_qkv(1).start()
+    for kind in range(3):
+        load_qkv(1, kind).start()
     load_out(1).start()
     finish_statistics(0)
     send_normed(0, lambda i: i)
     send_weights(1)
-    load_qkv(0).wait()
+    for kind in range(3):
+        load_qkv(0, kind).wait()
     own_product(0)
     spread_weights(0)
 
@@ -330,7 +336,8 @@
     lax.fori_loop(0, query_blocks, space_project, 0)
 
     send_statistics(1)
-    load_qkv(1).wait()
+    for kind in range(3):
+        load_qkv(1, kind).wait()
     finish_statistics(1)
 
     def time_order(i):
@@ -533,7 +540,7 @@
         pltpu.VMEM((2, parts, rows, part_width), bf16),
         pltpu.VMEM((parts, rows, heads_width), bf16),
         pltpu.VMEM((parts, frames, piece, heads_width), bf16),
-        dma, dma((2,)), dma((2,)), dma((2,)), dma((chunks,)),
+        dma, dma((2, 3)), dma((2,)), dma((2,)), dma((chunks,)),
         dma((2, parts)), dma((2, parts)),
         dma((2, parts, chunks)), dma((2, parts, chunks)),
         dma((chunks,)), dma((chunks,)),
@@ -559,8 +566,8 @@
             transcendentals=1024 * 1024,
         ),
     )(
-        block_mask, tokens, space_qkv.reshape(width, -1), space_out, space_mod,
-        time_qkv.reshape(width, -1), time_out, time_mod,
+        block_mask, tokens, jnp.swapaxes(space_qkv, 0, 1), space_out, space_mod,
+        jnp.swapaxes(time_qkv, 0, 1), time_out, time_mod,
     )
 
 

time: 130 us -> 106 us (0.82)
  local copies, waits for them, and re-layouts: 30 us -> 6.97 us
    reshape x2 -> x0, local copies, waits for them, and re-layouts: 13.5 us -> none  [the longest x1 6.82 us: on_device(): time_qkv.reshape(width, -1)]
    unnamed x12 -> x8, local copies, waits for them, and re-layouts: 16.5 us -> 6.97 us
where the time goes in v2:
time: 106 us
  Pallas kernels  98.9 us (93%)
  local copies, waits for them, and re-layouts  6.97 us (7%)
    pallas_call x1, Pallas kernels, on_device(): pl.pallas_call(functools.partial(sublayers, sizes), out_shape=jax.ShapeDt...  98.9 us
    unnamed x8, local copies, waits for them, and re-layouts  6.97 us

profile of v2, /device:TPU:0, one launch (start us, length us, event | category | flops | bytes accessed | tf_op | source)
XLA Modules:
  0.0 105.9 jit_solution(2912635302759922594)
XLA Ops:
  0.0 0.7 copy.9.mask_ref
  0.7 0.0 copy-start
  0.8 1.4 %copy-done = bf16[256,3072]{1,0:T(8,128)(2,1)S(1)} copy-done((bf16[256,3072]{1,0:T(8,128)(2,1)S(1)}, bf16[256,3072]{1,0:T(8,128)(2,1)}, u32[]{:S(2)}) %copy-start) | copy-done | bytes 1572888
  2.2 0.0 copy-start.1
  2.2 0.8 copy-done.1
  3.0 0.0 copy-start.2
  3.0 0.8 copy-done.2
  3.8 98.9 %shard_map.82 = f32[1,384,1536]{2,1,0:T(8,128)} custom-call(s32[8,6,6]{2,1,0:T(8,128)S(1)} %copy.9.mask_ref, f32[1,384,1536]{2,1,0:T(8,128)} %tokens_ref.1, bf16[3,3072,256]{2,1,0:T(8,128)(2,1)} %bitcast.2, bf16[256,3072]{1,0:T(8,128)(2,1)S(1)} %copy-done, f32[3,3072]{1,0:T(4,128)S(1)} %copy-done.1, bf16[3,3072,256]{2,1,0:T(8,128)(2,1)} %bitcast.3, ...), custom_call_target="tpu_custom_call" | custom-call | flops 4831838208 | bytes 20971520 | tf_op jit(solution)/shard_map/pallas_call | solution.py:555
  102.7 3.2 %copy.11 = f32[1,384,1536]{2,1,0:T(8,128)} copy(f32[1,384,1536]{2,1,0:T(8,128)} %shard_map.82) | data formatting | bytes 4718592
Async XLA Ops:
  0.7 1.4 %copy-start = (bf16[256,3072]{1,0:T(8,128)(2,1)S(1)}, bf16[256,3072]{1,0:T(8,128)(2,1)}, u32[]{:S(2)}) copy-start(bf16[256,3072]{1,0:T(8,128)(2,1)} %space_out_ref.1) | copy-start | bytes 4718596
  2.2 0.8 copy-start.1
  3.0 0.8 copy-start.2
